TPU v7x, 32 devices: a whole 2x2x4 slice. The times are simulated.
32 devices in a mesh: tm: 2 (over x), mesh: 16 (over z, y, core).
Axes of the slice: x: 2, y: 2, z: 4, core: 2. Of those that a mesh axis runs over, the one named last changes fastest.
Arguments:
- prev_ends: float32 [2, 1024, 1024], P('tm', 'mesh'), may hold values from -6 to 6
- initial: float32 [1024, 1024], P('mesh'), may hold values from -6 to 6
- source: float32 [2, 1024, 1024], P(None, 'mesh'), may hold values from -6 to 6
- region: int32 [1024, 1024], P('mesh'), may hold values from 0 to 3
- conductivity: float32 [4], replicated, may hold values from 0.05 to 2
- reluctivity: float32 [4], replicated, may hold values from 0.5 to 2
- saturation: float32 [4], replicated, may hold values from 0.05 to 0.5
Outputs:
- new_ends: float32 [2, 1024, 1024], P('tm', 'mesh')
All inputs are finite; a program needn't handle non-finite values.
Results may differ from a plain program's by a relative error of at most 0.0003.
Values sent between devices are 32-bit elements; how exact they have to be, the bound alone decides.
A program may use at most 64 MiB of HBM per device.

v0:
```python
import jax
import jax.numpy as jnp
from jax import lax
from jax.sharding import PartitionSpec as P

FSTEPS = 2
CG_ITERS = 5
REGIONS = 4


STEP_LENGTH = 1.0
FREQUENCY = 0.1
LUMPED = 0.02


def extended_2(x, sides, width):
    for axis, dim in sides:
        size, length = (lax.axis_size(axis), x.shape[dim])
        up = [(i, (i + 1) % size) for i in range(size - 1)]
        down = [(j, i) for i, j in up]
        last = lax.slice_in_dim(x, length - width, length, axis=dim)
        first = lax.slice_in_dim(x, 0, width, axis=dim)
        before = lax.ppermute(last, axis, up)
        after = lax.ppermute(first, axis, down)
        x = jnp.concatenate([before, x, after], axis=dim)
    return x


def passed_along(value, axis, steps):
    count = lax.axis_size(axis)
    first, last = (max(0, -steps), min(count, count - steps))
    return lax.ppermute(value, axis, [(source, source + steps) for source in range(first, last)])


def carried_in(x, axis, combine, identity):
    size, here = (lax.axis_size(axis), lax.axis_index(axis))
    everything = jax.tree.map(lambda part: lax.all_gather(part, axis), x)
    start = jax.tree.map(
        lambda part, zero: jnp.broadcast_to(jnp.asarray(zero, part.dtype), part.shape), x, identity
    )

    def turn(k, before):
        reached = k < here
        new = combine(before, jax.tree.map(lambda part: part[k], everything))
        return jax.tree.map(lambda a, b: jnp.where(reached, a, b), new, before)

    return lax.fori_loop(0, size, turn, start)


def lookup(region, values_table):
    summed = jnp.zeros(region.shape, values_table.dtype)
    for material in range(REGIONS):
        summed = summed + jnp.where(
            region == material, values_table[material], jnp.zeros((), values_table.dtype)
        )
    return summed


def reluctance(padded_rows, base_mid, slope_mid):
    padded = jnp.pad(padded_rows, ((0, 0), (1, 1)))
    grad_x = 0.5 * (padded[2:, 1:-1] - padded[:-2, 1:-1])
    grad_y = 0.5 * (padded[1:-1, 2:] - padded[1:-1, :-2])
    return base_mid * (1.0 + slope_mid * (grad_x * grad_x + grad_y * grad_y))


def stiffness(field_pad, weight_pad):
    middle = field_pad[1:-1, 1:-1]
    weight_mid = weight_pad[1:-1, 1:-1]
    summed = jnp.zeros_like(middle)
    cuts = (
        (slice(None, -2), slice(1, -1)),
        (slice(2, None), slice(1, -1)),
        (slice(1, -1), slice(None, -2)),
        (slice(1, -1), slice(2, None)),
    )
    for rows_cut, cols_cut in cuts:
        edge = 0.5 * (weight_mid + weight_pad[rows_cut, cols_cut])
        summed = summed + edge * (middle - field_pad[rows_cut, cols_cut])
    return summed


def operate(operand, weight_pad, conduct_step):
    rimmed = extended_2(operand, (("mesh", 0),), 1)
    field_pad = jnp.pad(rimmed, ((0, 0), (1, 1)))
    return conduct_step * operand + stiffness(field_pad, weight_pad)


def squares(residual):
    return lax.psum(jnp.sum(residual * residual), "mesh")


def fine_step(field_now, base_pad, slope_pad, conduct_step, current):
    extended = extended_2(field_now, (("mesh", 0),), 2)
    weights = reluctance(extended, base_pad, slope_pad)
    weight_pad = jnp.pad(weights, ((0, 0), (1, 1)))
    residual = current - stiffness(jnp.pad(extended[1:-1], ((0, 0), (1, 1))), weight_pad)
    iterate = field_now
    direction = residual
    norm_now = squares(residual)
    for sweep in range(CG_ITERS):
        image = operate(direction, weight_pad, conduct_step)
        step_size = norm_now / lax.psum(jnp.sum(direction * image), "mesh")
        iterate = iterate + step_size * direction
        residual = residual - step_size * image
        norm_next = squares(residual)
        direction = residual + norm_next / norm_now * direction
        norm_now = norm_next
    return iterate


def shards(prev_ends, initial, source, region, conductivity, reluctivity, saturation):
    shifted = passed_along(prev_ends, "tm", 1)
    slice_index = lax.axis_index("tm")
    first = slice_index == 0
    start = jnp.where(first, initial, shifted[0])
    conduct = lookup(region, conductivity)
    base = lookup(region, reluctivity)
    slope = lookup(region, saturation)
    stacked = extended_2(jnp.stack([base, slope]), (("mesh", 1),), 2)
    base_pad = stacked[0, 1:-1]
    slope_pad = stacked[1, 1:-1]
    conduct_step = conduct / STEP_LENGTH
    slice_time = slice_index.astype(jnp.float32)
    field_now = start
    for sweep in range(FSTEPS):
        moment = (slice_time * FSTEPS + sweep + 1) * STEP_LENGTH
        current = source[0] * jnp.cos(FREQUENCY * moment) + source[1] * jnp.sin(FREQUENCY * moment)
        field_now = fine_step(field_now, base_pad, slope_pad, conduct_step, current)
    decay = conduct / (conduct + LUMPED * base)
    decay_used = jnp.where(first, jnp.zeros_like(decay), decay)
    carried = field_now - decay_used * start

    def compose(earlier, later):
        return (later[0] * earlier[0], later[0] * earlier[1] + later[1])

    prefix = carried_in(
        (decay_used, carried), "tm", compose, (jnp.ones_like(decay), jnp.zeros_like(carried))
    )
    arrived = prefix[1]
    ended = decay_used * arrived + carried
    return ended[None]


def solution(mesh):
    in_specs = (
        P("tm", "mesh", None),
        P("mesh", None),
        P(None, "mesh", None),
        P("mesh", None),
        P(),
        P(),
        P(),
    )
    out_specs = P("tm", "mesh", None)
    return jax.shard_map(shards, mesh=mesh, in_specs=in_specs, out_specs=out_specs, check_vma=False)
```

profile of v0, /device:TPU:0, one launch (start us, length us, event | category | flops | bytes accessed | tf_op | source)
XLA Modules:
  0.0 736.7 jit_solution(2127794377353215536)
XLA Ops:
  0.0 4.8 collective-permute-start
  7.0 3.7 fusion.167
  17.8 5.2 collective-permute-start.4
  25.4 3.6 collective-permute-start.5
  34.0 3.4 multiply_reduce_fusion.16
  37.5 33.4 %all-reduce.17 = (f32[]{:T(128)}, f32[]{:T(128)}) all-reduce(f32[]{:T(128)} %get-tuple-element.121, f32[]{:T(128)} %get-tuple-element.120), channel_id=1, replica_groups=mesh['tm'=2,'mesh'=16] {'mesh'}, use_global_device_ids=true, to_apply=%region_1.2 | all-reduce | flops 2 | bytes 16 | tf_op jit(solution)/shard_map/psum | solution.py:89
  72.9 30.1 %psum.142 = f32[]{:T(128)} all-reduce(f32[]{:T(128)} %multiply_reduce_fusion.15), channel_id=1, replica_groups=mesh['tm'=2,'mesh'=16] {'mesh'}, use_global_device_ids=true, to_apply=%region_5.6 | all-reduce | flops 1 | bytes 8 | tf_op jit(solution)/shard_map/psum | solution.py:89
  109.4 3.4 multiply_reduce_fusion.14
  112.8 32.0 %psum.143 = f32[]{:T(128)} all-reduce(f32[]{:T(128)} %get-tuple-element.162), channel_id=1, replica_groups=mesh['tm'=2,'mesh'=16] {'mesh'}, use_global_device_ids=true, to_apply=%region_7.8 | all-reduce | flops 1 | bytes 8 | tf_op jit(solution)/shard_map/psum | solution.py:102
  146.9 30.2 %psum.144 = f32[]{:T(128)} all-reduce(f32[]{:T(128)} %get-tuple-element.160), channel_id=1, replica_groups=mesh['tm'=2,'mesh'=16] {'mesh'}, use_global_device_ids=true, to_apply=%region_9.10 | all-reduce | flops 1 | bytes 8 | tf_op jit(solution)/shard_map/psum | solution.py:89
  187.2 31.1 %psum.145 = f32[]{:T(128)} all-reduce(f32[]{:T(128)} %get-tuple-element.158), channel_id=1, replica_groups=mesh['tm'=2,'mesh'=16] {'mesh'}, use_global_device_ids=true, to_apply=%region_11.12 | all-reduce | flops 1 | bytes 8 | tf_op jit(solution)/shard_map/psum | solution.py:102
  220.4 30.1 %psum.146 = f32[]{:T(128)} all-reduce(f32[]{:T(128)} %get-tuple-element.156), channel_id=1, replica_groups=mesh['tm'=2,'mesh'=16] {'mesh'}, use_global_device_ids=true, to_apply=%region_13.14 | all-reduce | flops 1 | bytes 8 | tf_op jit(solution)/shard_map/psum | solution.py:89
  256.9 3.4 multiply_reduce_fusion.10
  260.3 32.0 %psum.147 = f32[]{:T(128)} all-reduce(f32[]{:T(128)} %get-tuple-element.154), channel_id=1, replica_groups=mesh['tm'=2,'mesh'=16] {'mesh'}, use_global_device_ids=true, to_apply=%region_15.16 | all-reduce | flops 1 | bytes 8 | tf_op jit(solution)/shard_map/psum | solution.py:102
  294.4 30.1 %psum.148 = f32[]{:T(128)} all-reduce(f32[]{:T(128)} %multiply_reduce_fusion.9), channel_id=1, replica_groups=mesh['tm'=2,'mesh'=16] {'mesh'}, use_global_device_ids=true, to_apply=%region_17.18 | all-reduce | flops 1 | bytes 8 | tf_op jit(solution)/shard_map/psum | solution.py:89
  330.9 3.4 fusion.117
  334.3 32.0 %psum.149 = f32[]{:T(128)} all-reduce(f32[]{:T(128)} %fusion.117), channel_id=1, replica_groups=mesh['tm'=2,'mesh'=16] {'mesh'}, use_global_device_ids=true, to_apply=%region_19.20 | all-reduce | flops 1 | bytes 8 | tf_op jit(solution)/shard_map/psum | solution.py:102
  381.5 3.5 multiply_reduce_fusion.7
  385.0 32.5 %all-reduce.16 = (f32[]{:T(128)}, f32[]{:T(128)}) all-reduce(f32[]{:T(128)} %get-tuple-element.119, f32[]{:T(128)} %get-tuple-element.118), channel_id=1, replica_groups=mesh['tm'=2,'mesh'=16] {'mesh'}, use_global_device_ids=true, to_apply=%region_21.22 | all-reduce | flops 2 | bytes 16 | tf_op jit(solution)/shard_map/psum | solution.py:89
  419.4 30.1 %psum.152 = f32[]{:T(128)} all-reduce(f32[]{:T(128)} %multiply_reduce_fusion.6), channel_id=1, replica_groups=mesh['tm'=2,'mesh'=16] {'mesh'}, use_global_device_ids=true, to_apply=%region_25.26 | all-reduce | flops 1 | bytes 8 | tf_op jit(solution)/shard_map/psum | solution.py:89
  455.8 3.5 multiply_reduce_fusion.5
  459.3 32.0 %psum.153 = f32[]{:T(128)} all-reduce(f32[]{:T(128)} %get-tuple-element.146), channel_id=1, replica_groups=mesh['tm'=2,'mesh'=16] {'mesh'}, use_global_device_ids=true, to_apply=%region_27.28 | all-reduce | flops 1 | bytes 8 | tf_op jit(solution)/shard_map/psum | solution.py:102
  493.3 30.1 %psum.154 = f32[]{:T(128)} all-reduce(f32[]{:T(128)} %get-tuple-element.144), channel_id=1, replica_groups=mesh['tm'=2,'mesh'=16] {'mesh'}, use_global_device_ids=true, to_apply=%region_29.30 | all-reduce | flops 1 | bytes 8 | tf_op jit(solution)/shard_map/psum | solution.py:89
  533.1 32.0 %psum.155 = f32[]{:T(128)} all-reduce(f32[]{:T(128)} %get-tuple-element.142), channel_id=1, replica_groups=mesh['tm'=2,'mesh'=16] {'mesh'}, use_global_device_ids=true, to_apply=%region_31.32 | all-reduce | flops 1 | bytes 8 | tf_op jit(solution)/shard_map/psum | solution.py:102
  567.0 30.1 %psum.156 = f32[]{:T(128)} all-reduce(f32[]{:T(128)} %get-tuple-element.140), channel_id=1, replica_groups=mesh['tm'=2,'mesh'=16] {'mesh'}, use_global_device_ids=true, to_apply=%region_33.34 | all-reduce | flops 1 | bytes 8 | tf_op jit(solution)/shard_map/psum | solution.py:89
  603.4 3.5 multiply_reduce_fusion.1
  606.9 32.0 %psum.157 = f32[]{:T(128)} all-reduce(f32[]{:T(128)} %get-tuple-element.138), channel_id=1, replica_groups=mesh['tm'=2,'mesh'=16] {'mesh'}, use_global_device_ids=true, to_apply=%region_35.36 | all-reduce | flops 1 | bytes 8 | tf_op jit(solution)/shard_map/psum | solution.py:102
  640.9 30.1 %psum.158 = f32[]{:T(128)} all-reduce(f32[]{:T(128)} %multiply_reduce_fusion), channel_id=1, replica_groups=mesh['tm'=2,'mesh'=16] {'mesh'}, use_global_device_ids=true, to_apply=%region_37.38 | all-reduce | flops 1 | bytes 8 | tf_op jit(solution)/shard_map/psum | solution.py:89
  681.8 32.0 %psum.159 = f32[]{:T(128)} all-reduce(f32[]{:T(128)} %fusion.63), channel_id=1, replica_groups=mesh['tm'=2,'mesh'=16] {'mesh'}, use_global_device_ids=true, to_apply=%region_39.40 | all-reduce | flops 1 | bytes 8 | tf_op jit(solution)/shard_map/psum | solution.py:102
  715.1 6.3 multiply_subtract_fusion
  721.5 7.0 all-gather.1
  728.5 7.0 all-gather
  (131 shorter events, 88.6 us)
Async XLA Ops:
  0.0 16.4 %collective-permute-start = (f32[1,64,1024]{2,1,0:T(8,128)}, f32[1,64,1024]{2,1,0:T(8,128)S(1)}, u32[]{:S(2)}, u32[]{:S(2)}) collective-permute-start(f32[1,64,1024]{2,1,0:T(8,128)} %param.9), channel_id=1, source_target_pairs={{0,16},{1,17},{2,18},{3,19},{4,20},{5,21},{6,22},{7,23},{8,24},{9,... | collective-permute-start | bytes 786440 | tf_op jit(solution)/shard_map/ppermute | solution.py:32
  13.3 3.1 copy-start.7
  13.4 9.7 %collective-permute-start.1 = (f32[2,2,1024]{2,1,0:T(2,128)S(1)}, f32[2,2,1024]{2,1,0:T(2,128)S(1)}, u32[]{:S(2)}, u32[]{:S(2)}) collective-permute-start(f32[2,2,1024]{2,1,0:T(2,128)S(1)} %get-tuple-element.175), channel_id=1, source_target_pairs={{0,1},{1,2},{2,3},{3,4},{4,5},{5,6},{6,7},{7,8},{8,9},{9,10},{10,1... | collective-permute-start | bytes 49160 | tf_op jit(solution)/shard_map/ppermute | solution.py:23
  15.0 8.1 %collective-permute-start.2 = (f32[2,2,1024]{2,1,0:T(2,128)S(1)}, f32[2,2,1024]{2,1,0:T(2,128)S(1)}, u32[]{:S(2)}, u32[]{:S(2)}) collective-permute-start(f32[2,2,1024]{2,1,0:T(2,128)S(1)} %get-tuple-element.176), channel_id=1, source_target_pairs={{1,0},{2,1},{3,2},{4,3},{5,4},{6,5},{7,6},{8,7},{9,8},{10,9},{11,1... | collective-permute-start | bytes 49160 | tf_op jit(solution)/shard_map/ppermute | solution.py:24
  16.5 6.7 collective-permute-start.3
  17.8 6.1 collective-permute-start.4
  25.4 4.9 copy-start.9
  25.4 5.5 collective-permute-start.5
  29.0 4.8 collective-permute-start.6
  104.4 3.1 collective-permute-start.7
  106.2 3.1 collective-permute-start.8
  178.5 4.3 collective-permute-start.10
  179.8 3.8 collective-permute-start.9
  251.9 3.1 collective-permute-start.11
  253.7 3.1 collective-permute-start.12
  325.9 3.1 collective-permute-start.13
  327.7 3.1 collective-permute-start.14
  367.8 5.3 copy-start.1
  367.8 4.6 collective-permute-start.15
  369.2 3.8 collective-permute-start.16
  374.6 3.6 collective-permute-start.17
  376.9 4.5 collective-permute-start.18
  450.8 3.1 collective-permute-start.19
  452.6 3.1 collective-permute-start.20
  524.7 3.1 collective-permute-start.21
  526.5 3.1 collective-permute-start.22
  598.4 3.1 collective-permute-start.23
  600.2 3.1 collective-permute-start.24
  606.9 65.5 %copy-start.2 = (f32[64,1024]{1,0:T(8,128)}, f32[64,1024]{1,0:T(8,128)S(1)}, u32[]{:S(2)}) copy-start(f32[64,1024]{1,0:T(8,128)S(1)} %get-tuple-element.139) | copy-start | bytes 786436
  672.5 3.1 collective-permute-start.25
  674.2 3.1 collective-permute-start.26
  675.5 2.9 copy-start.4
  (5 other events, 6.4 us)
where the time goes:
time: 739 us; the launch traced here: 737 us
  blocking collectives  576 us (78%)
  other arithmetic  58.2 us (8%)
  starting transfers between devices  52.9 us (7%)
  between operations  24.7 us (3%)
  waiting for transfers between devices  20.5 us (3%)
    psum x10, blocking collectives, squares(): return lax.psum(jnp.sum(residual * residual), 'mesh')  307 us
    psum x8, blocking collectives, fine_step(): step_size = norm_now / lax.psum(jnp.sum(direction * image), 'mesh')  255 us
    reduce_sum x10, other arithmetic, fine_step(): step_size = norm_now / lax.psum(jnp.sum(direction * image), 'mesh')  34.3 us
    ppermute x13, starting transfers between devices, extended_2(): before = lax.ppermute(last, axis, up)  31.1 us
    ppermute x13, waiting for transfers between devices, extended_2(): after = lax.ppermute(first, axis, down)  18.3 us
    ppermute x13, starting transfers between devices, extended_2(): after = lax.ppermute(first, axis, down)  16.9 us
  transfers between devices with their start and end apart: 27, of which 12 were waited for; matrix products, arithmetic and copies ran while one was open for 1% of the time, Pallas kernels for 0%

commit v1 on v0

v1 whole, which is shorter than its diff:
```python
import functools

import jax
import jax.numpy as jnp
from jax import lax
from jax.experimental import pallas as pl
from jax.experimental.pallas import tpu as pltpu
from jax.sharding import PartitionSpec as P

FSTEPS = 2
REGIONS = 4
STEP_LENGTH = 1.0
FREQUENCY = 0.1
LUMPED = 0.02
TILE = 8
HALO = 8
LANES = 128
CHUNKS = 4
MESH = pl.DeviceIdType.MESH
TINY = 3e-7


def folded(product):
    total = product[:, 0:LANES]
    for cut in range(1, product.shape[1] // LANES):
        total = total + product[:, cut * LANES : (cut + 1) * LANES]
    return total


def kernel(
    slices, n,
    prev_ref, initial_ref, source_ref, region_ref, con_tab, rel_tab, sat_tab,
    out_ref,
    u0, u1, reg, src, con, base, slope, wgt, diag, w_s, w_n, w_e, w_w,
    v0, v1, v2, v3, v4, carry, parts,
    local_sem, send_h, recv_h, send_p, recv_p, send_c, recv_c, send_s, recv_s,
):
    t = lax.axis_index("tm")
    m = lax.axis_index("mesh")
    rows, cols = initial_ref.shape
    tall = rows + 2 * HALO
    tiles = tall // TILE
    first, last = m == 0, m == n - 1
    inner = pl.ds(HALO, rows)

    loads = [
        pltpu.make_async_copy(region_ref, reg.at[inner], local_sem.at[0]),
        pltpu.make_async_copy(source_ref, src.at[:, inner], local_sem.at[1]),
    ]
    load_start = pltpu.make_async_copy(initial_ref, u0.at[inner], local_sem.at[2])
    for copy in loads:
        copy.start()

    @pl.when(t == 0)
    def _():
        load_start.start()

    barrier = pltpu.get_barrier_semaphore()
    for hop in range(1, n):
        pl.semaphore_signal(barrier, inc=1, device_id={"mesh": lax.rem(m + hop, n)}, device_id_type=MESH)

    @pl.when(t > 0)
    def _():
        pl.semaphore_signal(barrier, inc=1, device_id={"tm": t - 1}, device_id_type=MESH)

    @pl.when(t < slices - 1)
    def _():
        pl.semaphore_signal(barrier, inc=1, device_id={"tm": t + 1}, device_id_type=MESH)

    def blank(at):
        u0[at, :] = jnp.zeros((HALO, cols), jnp.float32)
        u1[at, :] = jnp.zeros((HALO, cols), jnp.float32)
        src[:, at, :] = jnp.zeros((2, HALO, cols), jnp.float32)
        reg[at, :] = jnp.full((HALO, cols), REGIONS, jnp.int32)

    top, bottom = pl.ds(0, HALO), pl.ds(HALO + rows, HALO)

    @pl.when(first)
    def _():
        blank(top)

    @pl.when(last)
    def _():
        blank(bottom)

    middle = (t > 0) & (t < slices - 1)

    @pl.when(middle)
    def _():
        pl.semaphore_wait(barrier, n + 1)

    @pl.when(jnp.logical_not(middle))
    def _():
        pl.semaphore_wait(barrier, n - 1 + min(slices - 1, 1))

    low, high = pl.ds(0, HALO), pl.ds(rows - HALO, HALO)
    own_low, own_high = pl.ds(HALO, HALO), pl.ds(rows, HALO)

    def halo(slot, up_src, up_dst, down_src, down_dst):
        up = pltpu.make_async_remote_copy(
            src_ref=up_src, dst_ref=up_dst, send_sem=send_h.at[2 * slot], recv_sem=recv_h.at[2 * slot],
            device_id={"mesh": m - 1}, device_id_type=MESH)
        down = pltpu.make_async_remote_copy(
            src_ref=down_src, dst_ref=down_dst, send_sem=send_h.at[2 * slot + 1], recv_sem=recv_h.at[2 * slot + 1],
            device_id={"mesh": m + 1}, device_id_type=MESH)
        return up, down

    halo_reg = halo(0, region_ref.at[low], reg.at[bottom], region_ref.at[high], reg.at[top])
    halo_src = halo(1, source_ref.at[:, low], src.at[:, bottom], source_ref.at[:, high], src.at[:, top])
    halo_first = halo(2, initial_ref.at[low], u0.at[bottom], initial_ref.at[high], u0.at[top])
    halo_later = halo(2, u0.at[own_low], u0.at[bottom], u0.at[own_high], u0.at[top])
    halo_next = halo(3, u1.at[own_low], u1.at[bottom], u1.at[own_high], u1.at[top])

    def start_up(pair):
        @pl.when(m > 0)
        def _():
            pair[0].start()

    def start_down(pair):
        @pl.when(m < n - 1)
        def _():
            pair[1].start()

    def arrive(pair):
        @pl.when(m < n - 1)
        def _():
            pair[0].wait_recv()

        @pl.when(m > 0)
        def _():
            pair[1].wait_recv()

    def sent(pair):
        @pl.when(m > 0)
        def _():
            pair[0].wait_send()

        @pl.when(m < n - 1)
        def _():
            pair[1].wait_send()

    pieces = []
    for k, (offset, length) in enumerate(((0, HALO), (rows - HALO, HALO), (HALO, rows - 2 * HALO))):
        pieces.append(pltpu.make_async_remote_copy(
            src_ref=prev_ref.at[0, pl.ds(offset, length)], dst_ref=u0.at[pl.ds(HALO + offset, length)],
            send_sem=send_p.at[k], recv_sem=recv_p.at[k], device_id={"tm": t + 1}, device_id_type=MESH))

    @pl.when(t < slices - 1)
    def _():
        for piece in pieces:
            piece.start()

    @pl.when(t == 0)
    def _():
        start_up(halo_first)
        start_down(halo_first)

    for pair in (halo_reg, halo_src):
        start_up(pair)
        start_down(pair)

    @pl.when(t > 0)
    def _():
        pieces[0].wait_recv()
        start_up(halo_later)
        pieces[1].wait_recv()
        start_down(halo_later)

    def at(k):
        return pl.ds(pl.multiple_of(k * TILE, TILE), TILE)

    sub = lax.broadcasted_iota(jnp.int32, (TILE, cols), 0)
    lane = lax.broadcasted_iota(jnp.int32, (TILE, cols), 1)

    def around(ref, k):
        here = ref[at(k), :]
        before = ref[at(lax.rem(k + tiles - 1, tiles)), :]
        after = ref[at(lax.rem(k + 1, tiles)), :]
        south = pltpu.roll(jnp.where(sub == 0, after, here), TILE - 1, 0)
        north = pltpu.roll(jnp.where(sub == TILE - 1, before, here), 1, 0)
        east = pltpu.roll(here, cols - 1, 1)
        west = pltpu.roll(here, 1, 1)
        return here, south, north, east, west

    def apply(ref, k):
        here, south, north, east, west = around(ref, k)
        image = (
            diag[at(k), :] * here
            - (w_s[at(k), :] * south + w_n[at(k), :] * north)
            - (w_e[at(k), :] * east + w_w[at(k), :] * west)
        )
        return here, image

    loads[0].wait()
    arrive(halo_reg)

    @pl.loop(0, tiles)
    def _(k):
        kind = reg[at(k), :]
        for table, into in ((con_tab, con), (rel_tab, base), (sat_tab, slope)):
            value = jnp.zeros((TILE, cols), jnp.float32)
            for material in range(REGIONS):
                value = jnp.where(kind == material, table[material], value)
            into[at(k), :] = value

    loads[1].wait()
    arrive(halo_src)

    @pl.when(t == 0)
    def _():
        load_start.wait()

    @pl.when(t > 0)
    def _():
        pieces[2].wait_recv()

    arrive(halo_first)

    def shared(slot, sums):
        for k, partial in enumerate(sums):
            parts[slot, m, k : k + 1, :] = jnp.sum(partial, axis=0, keepdims=True)
        for k in range(len(sums), TILE):
            parts[slot, m, k : k + 1, :] = jnp.zeros((1, LANES), jnp.float32)
        for hop in range(1, n):
            pltpu.make_async_remote_copy(
                src_ref=parts.at[slot, m], dst_ref=parts.at[slot, m],
                send_sem=send_s.at[slot], recv_sem=recv_s.at[slot],
                device_id={"mesh": lax.rem(m + hop, n)}, device_id_type=MESH).start()

    def everyone(slot, sem):
        return pltpu.make_async_copy(
            parts.at[slot, pl.ds(0, n - 1)], parts.at[slot, pl.ds(0, n - 1)], sem.at[slot])

    def gathered(slot, count):
        everyone(slot, recv_s).wait()
        total = parts[slot, 0]
        for other in range(1, n):
            total = total + parts[slot, other]
        summed = jnp.sum(total, axis=1, keepdims=True)
        return [summed[k : k + 1, :] for k in range(count)]

    def owned(k):
        return (k >= HALO // TILE) & (k < tiles - HALO // TILE)

    def zeros(count):
        return tuple(jnp.zeros((TILE, LANES), jnp.float32) for _ in range(count))

    def summed_up(k, sums, products):
        keep = jnp.where(owned(k), 1.0, 0.0)
        return tuple(s + keep * folded(p) for s, p in zip(sums, products))

    def fine_step(sweep, field, finish):
        moment = (t.astype(jnp.float32) * FSTEPS + sweep + 1) * STEP_LENGTH
        angle = jnp.full((1, 1), FREQUENCY * moment, jnp.float32)
        cosine, sine = jnp.cos(angle), jnp.sin(angle)

        @pl.loop(0, tiles)
        def _(k):
            here, south, north, east, west = around(field, k)
            east = jnp.where(lane == cols - 1, 0.0, east)
            west = jnp.where(lane == 0, 0.0, west)
            grad_x = 0.5 * (south - north)
            grad_y = 0.5 * (east - west)
            wgt[at(k), :] = base[at(k), :] * (1.0 + slope[at(k), :] * (grad_x * grad_x + grad_y * grad_y))

        @pl.loop(0, tiles)
        def _(k):
            here, south, north, east, west = around(wgt, k)
            east = 0.5 * (here + jnp.where(lane == cols - 1, 0.0, east))
            west = 0.5 * (here + jnp.where(lane == 0, 0.0, west))
            south = 0.5 * (here + south)
            north = 0.5 * (here + north)
            conduct = con[at(k), :]
            diag[at(k), :] = conduct + (south + north) + (east + west)
            row = m * rows + k * TILE - HALO + sub
            w_s[at(k), :] = jnp.where((row >= 0) & (row < n * rows - 1), south, 0.0)
            w_n[at(k), :] = jnp.where((row >= 1) & (row < n * rows), north, 0.0)
            w_e[at(k), :] = jnp.where(lane == cols - 1, 0.0, east)
            w_w[at(k), :] = jnp.where(lane == 0, 0.0, west)

        def residual(k, sums):
            here, image = apply(field, k)
            current = src[0, at(k), :] * cosine + src[1, at(k), :] * sine
            row = m * rows + k * TILE - HALO + sub
            value = current - (image - con[at(k), :] * here)
            value = jnp.where((row >= 0) & (row < n * rows), value, 0.0)
            v0[at(k), :] = value
            return summed_up(k, sums, (value * value,))

        (m0,) = lax.fori_loop(0, tiles, residual, zeros(1))

        def power_1(k, sums):
            here, image = apply(v0, k)
            v1[at(k), :] = image
            return summed_up(k, sums, (here * image, image * image))

        m1, m2 = lax.fori_loop(0, tiles, power_1, zeros(2))

        def power_2(k, sums):
            here, image = apply(v1, k)
            v2[at(k), :] = image
            return summed_up(k, sums, (here * image,))

        (m3,) = lax.fori_loop(0, tiles, power_2, zeros(1))
        shared(2 * sweep, (m0, m1, m2, m3))

        @pl.loop(0, tiles)
        def _(k):
            v3[at(k), :] = apply(v2, k)[1]

        @pl.loop(0, tiles)
        def _(k):
            v4[at(k), :] = apply(v3, k)[1]

        m0, m1, m2, m3 = gathered(2 * sweep, 4)
        a0 = m0 / m1
        rr1 = a0 * a0 * m2 - m0
        b0 = rr1 / m0
        g0 = 1.0 + b0
        pmp = g0 * g0 * m1 - 2.0 * g0 * a0 * m2 + a0 * a0 * m3
        a1 = rr1 / pmp
        ca = a0 + a1 * g0
        cb = a0 * a1

        def combine(k, sums):
            x1, x2, x3 = v1[at(k), :], v2[at(k), :], v3[at(k), :]
            r0 = v0[at(k), :] - ca * x1 + cb * x2
            r1 = x1 - ca * x2 + cb * x3
            r2 = x2 - ca * x3 + cb * v4[at(k), :]
            v2[at(k), :] = r0
            v3[at(k), :] = r1
            v4[at(k), :] = r2
            return summed_up(k, sums, (r0 * r0, r0 * r1, r1 * r1, r1 * r2, r2 * r2))

        h = lax.fori_loop(0, tiles, combine, zeros(5))

        def power_5(k, sums):
            here, image = apply(v4, k)
            return (sums[0] + folded(here * image),)

        (h5,) = lax.fori_loop(HALO // TILE, tiles - HALO // TILE, power_5, zeros(1))
        shared(2 * sweep + 1, h + (h5,))
        h0, h1, h2, h3, h4, h5 = gathered(2 * sweep + 1, 6)
        i0, i1 = 1.0 / a0, 1.0 / a1
        mix = i1 + b0 * i0
        q0 = -h0 * i1
        q1 = (q0 - h1) * i1
        q2 = (mix * q0 - h1 * i1 - h2) * i1
        f1 = -q0 * i0
        f2 = (-q0 * i0 + h1 * i1 - mix * q0) * i0
        ip, i_m = 1.0 / pmp, 1.0 / m1
        s00 = h1 - q0 * q0 * ip
        s01 = h2 - q0 * q1 * ip
        s02 = h3 - q0 * q2 * ip
        s11 = h3 - q1 * q1 * ip - f1 * f1 * i_m
        s12 = h4 - q1 * q2 * ip - f1 * f2 * i_m
        s22 = h5 - q2 * q2 * ip - f2 * f2 * i_m
        l10, l20 = s01 / s00, s02 / s00
        d1 = s11 - l10 * s01
        e12 = s12 - l10 * s02
        z1 = h1 - l10 * h0
        usable1 = d1 > TINY * h3
        l21 = jnp.where(usable1, e12 / d1, 0.0)
        d2 = s22 - l20 * s02 - l21 * e12
        z2 = h2 - l20 * h0 - l21 * z1
        y2 = jnp.where(usable1 & (d2 > TINY * h5), z2 / d2, 0.0)
        y1 = jnp.where(usable1, z1 / d1, 0.0) - l21 * y2
        y0 = h0 / s00 - l10 * y1 - l20 * y2
        c1 = -(y0 * q0 + y1 * q1 + y2 * q2) * ip
        c0 = -(y1 * f1 + y2 * f2) * i_m
        e0 = ca + c0 + c1 * g0
        e1 = -cb - c1 * a0

        def result(k):
            return (
                field[at(k), :] + (e0 * v0[at(k), :] + e1 * v1[at(k), :])
                + (y0 * v2[at(k), :] + y1 * v3[at(k), :] + y2 * v4[at(k), :])
            )

        finish(result)

    inside = (HALO // TILE, tiles - HALO // TILE)

    def between(result):
        u1[at(inside[0]), :] = result(inside[0])
        start_up(halo_next)
        u1[at(inside[1] - 1), :] = result(inside[1] - 1)
        start_down(halo_next)

        @pl.loop(inside[0] + 1, inside[1] - 1)
        def _(k):
            u1[at(k), :] = result(k)

        arrive(halo_next)

    span = rows // CHUNKS
    onward = [
        pltpu.make_async_remote_copy(
            src_ref=out_ref.at[0, pl.ds(c * span, span)], dst_ref=carry.at[pl.ds(c * span, span)],
            send_sem=send_c.at[c], recv_sem=recv_c.at[c], device_id={"tm": t + 1}, device_id_type=MESH)
        for c in range(CHUNKS)
    ]

    def final(result):
        @pl.when(t > 0)
        def _():
            @pl.loop(0, rows // TILE)
            def _(k):
                up = k + HALO // TILE
                conduct = con[at(up), :]
                decay = conduct / (conduct + LUMPED * base[at(up), :])
                wgt[at(k), :] = decay
                out_ref[0, at(k), :] = result(up) - decay * u0[at(up), :]

        for c in range(CHUNKS):
            @pl.when(t == 0)
            def _():
                @pl.loop(c * span // TILE, (c + 1) * span // TILE)
                def _(k):
                    out_ref[0, at(k), :] = result(k + HALO // TILE)

            @pl.when(t > 0)
            def _():
                onward[c].wait_recv()

                @pl.loop(c * span // TILE, (c + 1) * span // TILE)
                def _(k):
                    out_ref[0, at(k), :] = out_ref[0, at(k), :] + wgt[at(k), :] * carry[at(k), :]

            @pl.when(t < slices - 1)
            def _():
                onward[c].start()

    fine_step(0, u0, between)
    fine_step(1, u1, final)

    for pair in (halo_reg, halo_src, halo_first, halo_next):
        sent(pair)

    @pl.when(t < slices - 1)
    def _():
        for copy in pieces + onward:
            copy.wait_send()

    for slot in range(2 * FSTEPS):
        everyone(slot, send_s).wait()


def shards(slices, n, prev_ends, initial, source, region, conductivity, reluctivity, saturation):
    rows, cols = initial.shape
    tall = rows + 2 * HALO
    grid = pltpu.VMEM((tall, cols), jnp.float32)
    hbm = pl.BlockSpec(memory_space=pl.ANY)
    smem = pl.BlockSpec(memory_space=pltpu.SMEM)
    dma = pltpu.SemaphoreType.DMA
    return pl.pallas_call(
        functools.partial(kernel, slices, n),
        out_shape=jax.ShapeDtypeStruct((1, rows, cols), jnp.float32),
        in_specs=[hbm] * 4 + [smem] * 3,
        out_specs=pl.BlockSpec(memory_space=pltpu.VMEM),
        scratch_shapes=[
            grid, grid, pltpu.VMEM((tall, cols), jnp.int32), pltpu.VMEM((2, tall, cols), jnp.float32),
            *([grid] * 14),
            pltpu.VMEM((rows, cols), jnp.float32),
            pltpu.VMEM((2 * FSTEPS, n, TILE, LANES), jnp.float32),
            dma((3,)), dma((8,)), dma((8,)), dma((3,)), dma((3,)), dma((CHUNKS,)), dma((CHUNKS,)),
            dma((2 * FSTEPS,)), dma((2 * FSTEPS,)),
        ],
        compiler_params=pltpu.CompilerParams(
            collective_id=0, has_side_effects=True, vmem_limit_bytes=32 * 1024 * 1024),
    )(prev_ends, initial, source, region, conductivity, reluctivity, saturation)


def solution(mesh):
    in_specs = (
        P("tm", "mesh", None), P("mesh", None), P(None, "mesh", None), P("mesh", None), P(), P(), P(),
    )
    return jax.shard_map(
        functools.partial(shards, mesh.shape["tm"], mesh.shape["mesh"]),
        mesh=mesh, in_specs=in_specs, out_specs=P("tm", "mesh", None), check_vma=False)
```

time: 739 us -> 56.7 us (0.08)
  blocking collectives: 576 us -> 0 us
  other arithmetic: 58.2 us -> 0 us
  starting transfers between devices: 52.9 us -> 0 us
  Pallas kernels: 0 us -> 49.8 us
  between operations: 24.7 us -> 0.02 us
  waiting for transfers between devices: 20.5 us -> 0 us
    psum x18 -> x0, blocking collectives: 562 us -> none  [the longest x10 307 us: squares(): return lax.psum(jnp.sum(residual * residual), 'mesh')]
    ppermute x27 -> x0, starting transfers between devices: 52.9 us -> none  [the longest x13 31.1 us: extended_2(): before = lax.ppermute(last, axis, up)]
    pallas_call x0 -> x1, Pallas kernels: none -> 49.8 us  [shards(): pl.pallas_call(functools.partial(kernel, slices, n), out_shape=jax.ShapeD...]
    reduce_sum x18 -> x0, other arithmetic: 39.8 us -> none  [the longest x10 34.3 us: fine_step(): step_size = norm_now / lax.psum(jnp.sum(direction * image), 'mesh')]
    ppermute x27 -> x0, waiting for transfers between devices: 20.5 us -> none  [the longest x13 18.3 us: extended_2(): after = lax.ppermute(first, axis, down)]
    all_gather x2 -> x0, blocking collectives: 14.1 us -> none  [carried_in(): everything = jax.tree.map(lambda part: lax.all_gather(part, axis), x)]
  transfers between devices with their start and end apart: 27 -> 0, of which waited for: 12 -> 0; matrix products, arithmetic and copies ran while one was open for 1% -> 0% of each run, Pallas kernels for 0% -> 0%
where the time goes in v1:
time: 56.7 us; the launch traced here: 56.4 us
  Pallas kernels  49.8 us (88%)
  local copies, waits for them, and re-layouts  6.56 us (12%)
    pallas_call x1, Pallas kernels, shards(): pl.pallas_call(functools.partial(kernel, slices, n), out_shape=jax.ShapeD...  49.8 us
    unnamed x15, local copies, waits for them, and re-layouts  6.56 us

profile of v1, /device:TPU:0, one launch (start us, length us, event | category | flops | bytes accessed | tf_op | source)
XLA Modules:
  0.0 56.4 jit_solution(5480776505230987604)
XLA Ops:
  0.0 0.0 copy-start
  0.0 1.0 %copy-done = f32[2,64,1024]{2,1,0:T(8,128)S(1)} copy-done((f32[2,64,1024]{2,1,0:T(8,128)S(1)}, f32[2,64,1024]{2,1,0:T(8,128)}, u32[]{:S(2)}) %copy-start) | copy-done | bytes 524312
  1.0 0.0 copy-start.1
  1.0 0.9 %copy-done.1 = f32[1,64,1024]{2,1,0:T(8,128)S(1)} copy-done((f32[1,64,1024]{2,1,0:T(8,128)S(1)}, f32[1,64,1024]{2,1,0:T(8,128)}, u32[]{:S(2)}) %copy-start.1) | copy-done | bytes 262168
  2.0 0.0 copy-start.2
  2.0 0.9 %copy-done.2 = f32[64,1024]{1,0:T(8,128)S(1)} copy-done((f32[64,1024]{1,0:T(8,128)S(1)}, f32[64,1024]{1,0:T(8,128)}, u32[]{:S(2)}) %copy-start.2) | copy-done | bytes 262168
  2.9 0.0 copy-start.3
  2.9 0.9 %copy-done.3 = s32[64,1024]{1,0:T(8,128)S(1)} copy-done((s32[64,1024]{1,0:T(8,128)S(1)}, s32[64,1024]{1,0:T(8,128)}, u32[]{:S(2)}) %copy-start.3) | copy-done | bytes 262168
  3.9 0.0 copy-start.4
  3.9 0.7 %copy-done.4 = f32[4]{0:T(128)S(1)} copy-done((f32[4]{0:T(128)S(1)}, f32[4]{0:T(128)}, u32[]{:S(2)}) %copy-start.4) | copy-done | bytes 40
  4.5 0.0 copy-start.5
  4.6 0.7 %copy-done.5 = f32[4]{0:T(128)S(1)} copy-done((f32[4]{0:T(128)S(1)}, f32[4]{0:T(128)}, u32[]{:S(2)}) %copy-start.5) | copy-done | bytes 40
  5.2 0.0 copy-start.6
  5.2 0.7 %copy-done.6 = f32[4]{0:T(128)S(1)} copy-done((f32[4]{0:T(128)S(1)}, f32[4]{0:T(128)}, u32[]{:S(2)}) %copy-start.6) | copy-done | bytes 40
  5.9 49.8 %shard_map.73 = f32[1,64,1024]{2,1,0:T(8,128)S(1)} custom-call(f32[1,64,1024]{2,1,0:T(8,128)S(1)} %copy-done.1, f32[64,1024]{1,0:T(8,128)S(1)} %copy-done.2, f32[2,64,1024]{2,1,0:T(8,128)S(1)} %copy-done, s32[64,1024]{1,0:T(8,128)S(1)} %copy-done.3, f32[4]{0:T(128)S(1)} %copy-done.4, f32[4]{0:T(128)S(1)} %copy-done.5, f32[4]{0:T(128)S(1)} %copy-done.6), custom_call_target="tpu_custom_call" | custom-call | tf_op jit(solution)/shard_map/pallas_call | solution.py:456
  55.7 0.7 %copy.9 = f32[1,64,1024]{2,1,0:T(8,128)} copy(f32[1,64,1024]{2,1,0:T(8,128)S(1)} %shard_map.73) | data formatting | bytes 524288
Async XLA Ops:
  0.0 1.0 %copy-start = (f32[2,64,1024]{2,1,0:T(8,128)S(1)}, f32[2,64,1024]{2,1,0:T(8,128)}, u32[]{:S(2)}) copy-start(f32[2,64,1024]{2,1,0:T(8,128)} %source_ref.1) | copy-start | bytes 1572868
  1.0 0.9 %copy-start.1 = (f32[1,64,1024]{2,1,0:T(8,128)S(1)}, f32[1,64,1024]{2,1,0:T(8,128)}, u32[]{:S(2)}) copy-start(f32[1,64,1024]{2,1,0:T(8,128)} %prev_ref.1) | copy-start | bytes 786436
  2.0 0.9 %copy-start.2 = (f32[64,1024]{1,0:T(8,128)S(1)}, f32[64,1024]{1,0:T(8,128)}, u32[]{:S(2)}) copy-start(f32[64,1024]{1,0:T(8,128)} %initial_ref.1) | copy-start | bytes 786436
  2.9 0.9 %copy-start.3 = (s32[64,1024]{1,0:T(8,128)S(1)}, s32[64,1024]{1,0:T(8,128)}, u32[]{:S(2)}) copy-start(s32[64,1024]{1,0:T(8,128)} %region_ref.1) | copy-start | bytes 786436
  3.9 0.7 %copy-start.4 = (f32[4]{0:T(128)S(1)}, f32[4]{0:T(128)}, u32[]{:S(2)}) copy-start(f32[4]{0:T(128)} %con_tab.1) | copy-start | bytes 52
  4.5 0.7 %copy-start.5 = (f32[4]{0:T(128)S(1)}, f32[4]{0:T(128)}, u32[]{:S(2)}) copy-start(f32[4]{0:T(128)} %rel_tab.1) | copy-start | bytes 52
  5.2 0.7 %copy-start.6 = (f32[4]{0:T(128)S(1)}, f32[4]{0:T(128)}, u32[]{:S(2)}) copy-start(f32[4]{0:T(128)} %sat_tab.1) | copy-start | bytes 52

commit v2 on v1

--- a/solution.py
+++ b/solution.py
@@ -29,10 +29,10 @@
 
 def kernel(
     slices, n,
-    prev_ref, initial_ref, source_ref, region_ref, con_tab, rel_tab, sat_tab,
+    prev_ref, initial_ref, source_ref, region_ref, con_ref, rel_ref, sat_ref,
     out_ref,
     u0, u1, reg, src, con, base, slope, wgt, diag, w_s, w_n, w_e, w_w,
-    v0, v1, v2, v3, v4, carry, parts,
+    v0, v1, v2, v3, v4, carry, parts, con_tab, rel_tab, sat_tab,
     local_sem, send_h, recv_h, send_p, recv_p, send_c, recv_c, send_s, recv_s,
 ):
     t = lax.axis_index("tm")
@@ -46,6 +46,9 @@
     loads = [
         pltpu.make_async_copy(region_ref, reg.at[inner], local_sem.at[0]),
         pltpu.make_async_copy(source_ref, src.at[:, inner], local_sem.at[1]),
+        pltpu.make_async_copy(con_ref, con_tab, local_sem.at[3]),
+        pltpu.make_async_copy(rel_ref, rel_tab, local_sem.at[4]),
+        pltpu.make_async_copy(sat_ref, sat_tab, local_sem.at[5]),
     ]
     load_start = pltpu.make_async_copy(initial_ref, u0.at[inner], local_sem.at[2])
     for copy in loads:
@@ -192,9 +195,11 @@
         return here, image
 
     loads[0].wait()
+    for copy in loads[2:]:
+        copy.wait()
     arrive(halo_reg)
 
-    @pl.loop(0, tiles)
+    @pl.loop(0, tiles, unroll=10)
     def _(k):
         kind = reg[at(k), :]
         for table, into in ((con_tab, con), (rel_tab, base), (sat_tab, slope)):
@@ -254,7 +259,7 @@
         angle = jnp.full((1, 1), FREQUENCY * moment, jnp.float32)
         cosine, sine = jnp.cos(angle), jnp.sin(angle)
 
-        @pl.loop(0, tiles)
+        @pl.loop(0, tiles, unroll=10)
         def _(k):
             here, south, north, east, west = around(field, k)
             east = jnp.where(lane == cols - 1, 0.0, east)
@@ -263,7 +268,7 @@
             grad_y = 0.5 * (east - west)
             wgt[at(k), :] = base[at(k), :] * (1.0 + slope[at(k), :] * (grad_x * grad_x + grad_y * grad_y))
 
-        @pl.loop(0, tiles)
+        @pl.loop(0, tiles, unroll=10)
         def _(k):
             here, south, north, east, west = around(wgt, k)
             east = 0.5 * (here + jnp.where(lane == cols - 1, 0.0, east))
@@ -287,28 +292,28 @@
             v0[at(k), :] = value
             return summed_up(k, sums, (value * value,))
 
-        (m0,) = lax.fori_loop(0, tiles, residual, zeros(1))
+        (m0,) = lax.fori_loop(0, tiles, residual, zeros(1), unroll=10)
 
         def power_1(k, sums):
             here, image = apply(v0, k)
             v1[at(k), :] = image
             return summed_up(k, sums, (here * image, image * image))
 
-        m1, m2 = lax.fori_loop(0, tiles, power_1, zeros(2))
+        m1, m2 = lax.fori_loop(0, tiles, power_1, zeros(2), unroll=10)
 
         def power_2(k, sums):
             here, image = apply(v1, k)
             v2[at(k), :] = image
             return summed_up(k, sums, (here * image,))
 
-        (m3,) = lax.fori_loop(0, tiles, power_2, zeros(1))
+        (m3,) = lax.fori_loop(0, tiles, power_2, zeros(1), unroll=10)
         shared(2 * sweep, (m0, m1, m2, m3))
 
-        @pl.loop(0, tiles)
+        @pl.loop(0, tiles, unroll=10)
         def _(k):
             v3[at(k), :] = apply(v2, k)[1]
 
-        @pl.loop(0, tiles)
+        @pl.loop(0, tiles, unroll=10)
         def _(k):
             v4[at(k), :] = apply(v3, k)[1]
 
@@ -332,7 +337,7 @@
             v4[at(k), :] = r2
             return summed_up(k, sums, (r0 * r0, r0 * r1, r1 * r1, r1 * r2, r2 * r2))
 
-        h = lax.fori_loop(0, tiles, combine, zeros(5))
+        h = lax.fori_loop(0, tiles, combine, zeros(5), unroll=10)
 
         def power_5(k, sums):
             here, image = apply(v4, k)
@@ -450,20 +455,20 @@
     rows, cols = initial.shape
     tall = rows + 2 * HALO
     grid = pltpu.VMEM((tall, cols), jnp.float32)
-    hbm = pl.BlockSpec(memory_space=pl.ANY)
-    smem = pl.BlockSpec(memory_space=pltpu.SMEM)
+    hbm = pl.BlockSpec(memory_space=pltpu.HBM)
     dma = pltpu.SemaphoreType.DMA
     return pl.pallas_call(
         functools.partial(kernel, slices, n),
         out_shape=jax.ShapeDtypeStruct((1, rows, cols), jnp.float32),
-        in_specs=[hbm] * 4 + [smem] * 3,
+        in_specs=[hbm] * 7,
         out_specs=pl.BlockSpec(memory_space=pltpu.VMEM),
         scratch_shapes=[
             grid, grid, pltpu.VMEM((tall, cols), jnp.int32), pltpu.VMEM((2, tall, cols), jnp.float32),
             *([grid] * 14),
             pltpu.VMEM((rows, cols), jnp.float32),
             pltpu.VMEM((2 * FSTEPS, n, TILE, LANES), jnp.float32),
-            dma((3,)), dma((8,)), dma((8,)), dma((3,)), dma((3,)), dma((CHUNKS,)), dma((CHUNKS,)),
+            *([pltpu.SMEM((REGIONS,), jnp.float32)] * 3),
+            dma((6,)), dma((8,)), dma((8,)), dma((3,)), dma((3,)), dma((CHUNKS,)), dma((CHUNKS,)),
             dma((2 * FSTEPS,)), dma((2 * FSTEPS,)),
         ],
         compiler_params=pltpu.CompilerParams(

time: 56.7 us -> 48.5 us (0.86)
  Pallas kernels: 49.8 us -> 41.6 us
    pallas_call x1, Pallas kernels: 49.8 us -> 41.6 us  [shards(): pl.pallas_call(functools.partial(kernel, slices, n), out_shape=jax.ShapeD...]
where the time goes in v2:
time: 48.5 us; the launch traced here: 48.2 us
  Pallas kernels  41.6 us (86%)
  local copies, waits for them, and re-layouts  6.56 us (14%)
    pallas_call x1, Pallas kernels, shards(): pl.pallas_call(functools.partial(kernel, slices, n), out_shape=jax.ShapeD...  41.6 us
    unnamed x15, local copies, waits for them, and re-layouts  6.56 us

profile of v2, /device:TPU:0, one launch (start us, length us, event | category | flops | bytes accessed | tf_op | source)
XLA Modules:
  0.0 48.2 jit_solution(6771238149406138186)
XLA Ops:
  0.0 0.0 copy-start
  0.0 1.0 %copy-done = f32[2,64,1024]{2,1,0:T(8,128)S(1)} copy-done((f32[2,64,1024]{2,1,0:T(8,128)S(1)}, f32[2,64,1024]{2,1,0:T(8,128)}, u32[]{:S(2)}) %copy-start) | copy-done | bytes 524312
  1.0 0.0 copy-start.1
  1.0 0.9 %copy-done.1 = f32[1,64,1024]{2,1,0:T(8,128)S(1)} copy-done((f32[1,64,1024]{2,1,0:T(8,128)S(1)}, f32[1,64,1024]{2,1,0:T(8,128)}, u32[]{:S(2)}) %copy-start.1) | copy-done | bytes 262168
  2.0 0.0 copy-start.2
  2.0 0.9 %copy-done.2 = f32[64,1024]{1,0:T(8,128)S(1)} copy-done((f32[64,1024]{1,0:T(8,128)S(1)}, f32[64,1024]{1,0:T(8,128)}, u32[]{:S(2)}) %copy-start.2) | copy-done | bytes 262168
  2.9 0.0 copy-start.3
  2.9 0.9 %copy-done.3 = s32[64,1024]{1,0:T(8,128)S(1)} copy-done((s32[64,1024]{1,0:T(8,128)S(1)}, s32[64,1024]{1,0:T(8,128)}, u32[]{:S(2)}) %copy-start.3) | copy-done | bytes 262168
  3.9 0.0 copy-start.4
  3.9 0.7 %copy-done.4 = f32[4]{0:T(128)S(1)} copy-done((f32[4]{0:T(128)S(1)}, f32[4]{0:T(128)}, u32[]{:S(2)}) %copy-start.4) | copy-done | bytes 40
  4.5 0.0 copy-start.5
  4.6 0.7 %copy-done.5 = f32[4]{0:T(128)S(1)} copy-done((f32[4]{0:T(128)S(1)}, f32[4]{0:T(128)}, u32[]{:S(2)}) %copy-start.5) | copy-done | bytes 40
  5.2 0.0 copy-start.6
  5.2 0.7 %copy-done.6 = f32[4]{0:T(128)S(1)} copy-done((f32[4]{0:T(128)S(1)}, f32[4]{0:T(128)}, u32[]{:S(2)}) %copy-start.6) | copy-done | bytes 40
  5.9 41.6 %shard_map.73 = f32[1,64,1024]{2,1,0:T(8,128)S(1)} custom-call(f32[1,64,1024]{2,1,0:T(8,128)S(1)} %copy-done.1, f32[64,1024]{1,0:T(8,128)S(1)} %copy-done.2, f32[2,64,1024]{2,1,0:T(8,128)S(1)} %copy-done, s32[64,1024]{1,0:T(8,128)S(1)} %copy-done.3, f32[4]{0:T(128)S(1)} %copy-done.4, f32[4]{0:T(128)S(1)} %copy-done.5, f32[4]{0:T(128)S(1)} %copy-done.6), custom_call_target="tpu_custom_call" | custom-call | tf_op jit(solution)/shard_map/pallas_call | solution.py:460
  47.5 0.7 %copy.9 = f32[1,64,1024]{2,1,0:T(8,128)} copy(f32[1,64,1024]{2,1,0:T(8,128)S(1)} %shard_map.73) | data formatting | bytes 524288
Async XLA Ops:
  0.0 1.0 %copy-start = (f32[2,64,1024]{2,1,0:T(8,128)S(1)}, f32[2,64,1024]{2,1,0:T(8,128)}, u32[]{:S(2)}) copy-start(f32[2,64,1024]{2,1,0:T(8,128)} %source_ref.1) | copy-start | bytes 1572868
  1.0 0.9 %copy-start.1 = (f32[1,64,1024]{2,1,0:T(8,128)S(1)}, f32[1,64,1024]{2,1,0:T(8,128)}, u32[]{:S(2)}) copy-start(f32[1,64,1024]{2,1,0:T(8,128)} %prev_ref.1) | copy-start | bytes 786436
  2.0 0.9 %copy-start.2 = (f32[64,1024]{1,0:T(8,128)S(1)}, f32[64,1024]{1,0:T(8,128)}, u32[]{:S(2)}) copy-start(f32[64,1024]{1,0:T(8,128)} %initial_ref.1) | copy-start | bytes 786436
  2.9 0.9 %copy-start.3 = (s32[64,1024]{1,0:T(8,128)S(1)}, s32[64,1024]{1,0:T(8,128)}, u32[]{:S(2)}) copy-start(s32[64,1024]{1,0:T(8,128)} %region_ref.1) | copy-start | bytes 786436
  3.9 0.7 %copy-start.4 = (f32[4]{0:T(128)S(1)}, f32[4]{0:T(128)}, u32[]{:S(2)}) copy-start(f32[4]{0:T(128)} %con_ref.1) | copy-start | bytes 52
  4.5 0.7 %copy-start.5 = (f32[4]{0:T(128)S(1)}, f32[4]{0:T(128)}, u32[]{:S(2)}) copy-start(f32[4]{0:T(128)} %rel_ref.1) | copy-start | bytes 52
  5.2 0.7 %copy-start.6 = (f32[4]{0:T(128)S(1)}, f32[4]{0:T(128)}, u32[]{:S(2)}) copy-start(f32[4]{0:T(128)} %sat_ref.1) | copy-start | bytes 52

commit v3 on v2

--- a/solution.py
+++ b/solution.py
@@ -199,7 +199,7 @@
         copy.wait()
     arrive(halo_reg)
 
-    @pl.loop(0, tiles, unroll=10)
+    @pl.loop(0, tiles, unroll=tiles)
     def _(k):
         kind = reg[at(k), :]
         for table, into in ((con_tab, con), (rel_tab, base), (sat_tab, slope)):
@@ -209,7 +209,6 @@
             into[at(k), :] = value
 
     loads[1].wait()
-    arrive(halo_src)
 
     @pl.when(t == 0)
     def _():
@@ -219,7 +218,12 @@
     def _():
         pieces[2].wait_recv()
 
-    arrive(halo_first)
+    def first_halos():
+        arrive(halo_src)
+        arrive(halo_first)
+
+    def later_halos():
+        arrive(halo_next)
 
     def shared(slot, sums):
         for k, partial in enumerate(sums):
@@ -254,22 +258,21 @@
         keep = jnp.where(owned(k), 1.0, 0.0)
         return tuple(s + keep * folded(p) for s, p in zip(sums, products))
 
-    def fine_step(sweep, field, finish):
+    def fine_step(sweep, field, arrived, idle, finish):
         moment = (t.astype(jnp.float32) * FSTEPS + sweep + 1) * STEP_LENGTH
         angle = jnp.full((1, 1), FREQUENCY * moment, jnp.float32)
         cosine, sine = jnp.cos(angle), jnp.sin(angle)
 
-        @pl.loop(0, tiles, unroll=10)
-        def _(k):
+        def weights(k, sums):
             here, south, north, east, west = around(field, k)
             east = jnp.where(lane == cols - 1, 0.0, east)
             west = jnp.where(lane == 0, 0.0, west)
             grad_x = 0.5 * (south - north)
             grad_y = 0.5 * (east - west)
             wgt[at(k), :] = base[at(k), :] * (1.0 + slope[at(k), :] * (grad_x * grad_x + grad_y * grad_y))
-
-        @pl.loop(0, tiles, unroll=10)
-        def _(k):
+            return sums
+
+        def edges(k, sums):
             here, south, north, east, west = around(wgt, k)
             east = 0.5 * (here + jnp.where(lane == cols - 1, 0.0, east))
             west = 0.5 * (here + jnp.where(lane == 0, 0.0, west))
@@ -282,6 +285,7 @@
             w_n[at(k), :] = jnp.where((row >= 1) & (row < n * rows), north, 0.0)
             w_e[at(k), :] = jnp.where(lane == cols - 1, 0.0, east)
             w_w[at(k), :] = jnp.where(lane == 0, 0.0, west)
+            return sums
 
         def residual(k, sums):
             here, image = apply(field, k)
@@ -292,28 +296,37 @@
             v0[at(k), :] = value
             return summed_up(k, sums, (value * value,))
 
-        (m0,) = lax.fori_loop(0, tiles, residual, zeros(1), unroll=10)
+        low, high = HALO // TILE + 1, tiles - HALO // TILE - 1
+        plan = ((weights, low, high), (edges, low + 1, high - 1), (residual, low + 1, high - 1))
+        sums = zeros(1)
+        for work, begin, end in plan:
+            sums = lax.fori_loop(begin, end, work, sums, unroll=end - begin)
+        arrived()
+        for work, begin, end in plan:
+            for k in (*range(begin), *range(end, tiles)):
+                sums = work(k, sums)
+        (m0,) = sums
 
         def power_1(k, sums):
             here, image = apply(v0, k)
             v1[at(k), :] = image
             return summed_up(k, sums, (here * image, image * image))
 
-        m1, m2 = lax.fori_loop(0, tiles, power_1, zeros(2), unroll=10)
+        m1, m2 = lax.fori_loop(0, tiles, power_1, zeros(2), unroll=tiles)
 
         def power_2(k, sums):
             here, image = apply(v1, k)
             v2[at(k), :] = image
             return summed_up(k, sums, (here * image,))
 
-        (m3,) = lax.fori_loop(0, tiles, power_2, zeros(1), unroll=10)
+        (m3,) = lax.fori_loop(0, tiles, power_2, zeros(1), unroll=tiles)
         shared(2 * sweep, (m0, m1, m2, m3))
 
-        @pl.loop(0, tiles, unroll=10)
+        @pl.loop(0, tiles, unroll=tiles)
         def _(k):
             v3[at(k), :] = apply(v2, k)[1]
 
-        @pl.loop(0, tiles, unroll=10)
+        @pl.loop(0, tiles, unroll=tiles)
         def _(k):
             v4[at(k), :] = apply(v3, k)[1]
 
@@ -337,14 +350,16 @@
             v4[at(k), :] = r2
             return summed_up(k, sums, (r0 * r0, r0 * r1, r1 * r1, r1 * r2, r2 * r2))
 
-        h = lax.fori_loop(0, tiles, combine, zeros(5), unroll=10)
+        h = lax.fori_loop(0, tiles, combine, zeros(5), unroll=tiles)
 
         def power_5(k, sums):
             here, image = apply(v4, k)
             return (sums[0] + folded(here * image),)
 
-        (h5,) = lax.fori_loop(HALO // TILE, tiles - HALO // TILE, power_5, zeros(1))
+        (h5,) = lax.fori_loop(
+            HALO // TILE, tiles - HALO // TILE, power_5, zeros(1), unroll=rows // TILE)
         shared(2 * sweep + 1, h + (h5,))
+        idle()
         h0, h1, h2, h3, h4, h5 = gathered(2 * sweep + 1, 6)
         i0, i1 = 1.0 / a0, 1.0 / a1
         mix = i1 + b0 * i0
@@ -392,11 +407,9 @@
         u1[at(inside[1] - 1), :] = result(inside[1] - 1)
         start_down(halo_next)
 
-        @pl.loop(inside[0] + 1, inside[1] - 1)
+        @pl.loop(inside[0] + 1, inside[1] - 1, unroll=inside[1] - inside[0] - 2)
         def _(k):
             u1[at(k), :] = result(k)
-
-        arrive(halo_next)
 
     span = rows // CHUNKS
     onward = [
@@ -406,21 +419,30 @@
         for c in range(CHUNKS)
     ]
 
-    def final(result):
+    def decays():
+        sent(halo_next)
+
         @pl.when(t > 0)
         def _():
-            @pl.loop(0, rows // TILE)
+            @pl.loop(0, rows // TILE, unroll=rows // TILE)
             def _(k):
                 up = k + HALO // TILE
                 conduct = con[at(up), :]
                 decay = conduct / (conduct + LUMPED * base[at(up), :])
                 wgt[at(k), :] = decay
-                out_ref[0, at(k), :] = result(up) - decay * u0[at(up), :]
+                u1[at(up), :] = u1[at(up), :] - decay * u0[at(up), :]
+
+    def final(result):
+        @pl.when(t > 0)
+        def _():
+            @pl.loop(0, rows // TILE, unroll=rows // TILE)
+            def _(k):
+                out_ref[0, at(k), :] = result(k + HALO // TILE)
 
         for c in range(CHUNKS):
             @pl.when(t == 0)
             def _():
-                @pl.loop(c * span // TILE, (c + 1) * span // TILE)
+                @pl.loop(c * span // TILE, (c + 1) * span // TILE, unroll=span // TILE)
                 def _(k):
                     out_ref[0, at(k), :] = result(k + HALO // TILE)
 
@@ -428,7 +450,7 @@
             def _():
                 onward[c].wait_recv()
 
-                @pl.loop(c * span // TILE, (c + 1) * span // TILE)
+                @pl.loop(c * span // TILE, (c + 1) * span // TILE, unroll=span // TILE)
                 def _(k):
                     out_ref[0, at(k), :] = out_ref[0, at(k), :] + wgt[at(k), :] * carry[at(k), :]
 
@@ -436,10 +458,10 @@
             def _():
                 onward[c].start()
 
-    fine_step(0, u0, between)
-    fine_step(1, u1, final)
-
-    for pair in (halo_reg, halo_src, halo_first, halo_next):
+    fine_step(0, u0, first_halos, lambda: None, between)
+    fine_step(1, u1, later_halos, decays, final)
+
+    for pair in (halo_reg, halo_src, halo_first):
         sent(pair)
 
     @pl.when(t < slices - 1)
@@ -472,7 +494,7 @@
             dma((2 * FSTEPS,)), dma((2 * FSTEPS,)),
         ],
         compiler_params=pltpu.CompilerParams(
-            collective_id=0, has_side_effects=True, vmem_limit_bytes=32 * 1024 * 1024),
+            collective_id=0, has_side_effects=True, vmem_limit_bytes=63 * 1024 * 1024),
     )(prev_ends, initial, source, region, conductivity, reluctivity, saturation)
 
 

time: 48.5 us -> 42.4 us (0.87)
  local copies, waits for them, and re-layouts: 6.56 us -> 1.67 us
  Pallas kernels: 41.6 us -> 40.6 us
    unnamed x15 -> x1, local copies, waits for them, and re-layouts: 6.56 us -> 1.67 us
    pallas_call x1, Pallas kernels: 41.6 us -> 40.6 us  [shards(): pl.pallas_call(functools.partial(kernel, slices, n), out_shape=jax.ShapeD...]
where the time goes in v3:
time: 42.4 us; the launch traced here: 42.3 us
  Pallas kernels  40.6 us (96%)
  local copies, waits for them, and re-layouts  1.67 us (4%)
    pallas_call x1, Pallas kernels, shards(): pl.pallas_call(functools.partial(kernel, slices, n), out_shape=jax.ShapeD...  40.6 us
    unnamed x1, local copies, waits for them, and re-layouts  1.67 us

profile of v3, /device:TPU:0, one launch (start us, length us, event | category | flops | bytes accessed | tf_op | source)
XLA Modules:
  0.0 42.3 jit_solution(7085524297772043557)
XLA Ops:
  0.0 40.6 %shard_map.73 = f32[1,64,1024]{2,1,0:T(8,128)} custom-call(f32[1,64,1024]{2,1,0:T(8,128)} %prev_ref.1, f32[64,1024]{1,0:T(8,128)} %initial_ref.1, f32[2,64,1024]{2,1,0:T(8,128)} %source_ref.1, s32[64,1024]{1,0:T(8,128)} %region_ref.1, f32[4]{0:T(128)} %con_ref.1, f32[4]{0:T(128)} %rel_ref.1, f32[4]{0:T(128)} %sat_ref.1), custom_call_target="tpu_custom_call" | custom-call | tf_op jit(solution)/shard_map/pallas_call | solution.py:482
  40.6 1.7 %copy.9 = f32[1,64,1024]{2,1,0:T(8,128)} copy(f32[1,64,1024]{2,1,0:T(8,128)} %shard_map.73) | data formatting | bytes 524288

commit v4 on v3

--- a/solution.py
+++ b/solution.py
@@ -31,7 +31,7 @@
     slices, n,
     prev_ref, initial_ref, source_ref, region_ref, con_ref, rel_ref, sat_ref,
     out_ref,
-    u0, u1, reg, src, con, base, slope, wgt, diag, w_s, w_n, w_e, w_w,
+    stage, u0, u1, reg, src, con, base, slope, wgt, diag, w_s, w_n, w_e, w_w,
     v0, v1, v2, v3, v4, carry, parts, con_tab, rel_tab, sat_tab,
     local_sem, send_h, recv_h, send_p, recv_p, send_c, recv_c, send_s, recv_s,
 ):
@@ -230,7 +230,7 @@
             parts[slot, m, k : k + 1, :] = jnp.sum(partial, axis=0, keepdims=True)
         for k in range(len(sums), TILE):
             parts[slot, m, k : k + 1, :] = jnp.zeros((1, LANES), jnp.float32)
-        for hop in range(1, n):
+        for hop in sorted(range(1, n), key=lambda h: -min(h, n - h)):
             pltpu.make_async_remote_copy(
                 src_ref=parts.at[slot, m], dst_ref=parts.at[slot, m],
                 send_sem=send_s.at[slot], recv_sem=recv_s.at[slot],
@@ -414,8 +414,14 @@
     span = rows // CHUNKS
     onward = [
         pltpu.make_async_remote_copy(
-            src_ref=out_ref.at[0, pl.ds(c * span, span)], dst_ref=carry.at[pl.ds(c * span, span)],
+            src_ref=stage.at[0, pl.ds(c * span, span)], dst_ref=carry.at[pl.ds(c * span, span)],
             send_sem=send_c.at[c], recv_sem=recv_c.at[c], device_id={"tm": t + 1}, device_id_type=MESH)
+        for c in range(CHUNKS)
+    ]
+
+    stores = [
+        pltpu.make_async_copy(
+            stage.at[0, pl.ds(c * span, span)], out_ref.at[0, pl.ds(c * span, span)], local_sem.at[6 + c])
         for c in range(CHUNKS)
     ]
 
@@ -437,14 +443,14 @@
         def _():
             @pl.loop(0, rows // TILE, unroll=rows // TILE)
             def _(k):
-                out_ref[0, at(k), :] = result(k + HALO // TILE)
+                stage[0, at(k), :] = result(k + HALO // TILE)
 
         for c in range(CHUNKS):
             @pl.when(t == 0)
             def _():
                 @pl.loop(c * span // TILE, (c + 1) * span // TILE, unroll=span // TILE)
                 def _(k):
-                    out_ref[0, at(k), :] = result(k + HALO // TILE)
+                    stage[0, at(k), :] = result(k + HALO // TILE)
 
             @pl.when(t > 0)
             def _():
@@ -452,12 +458,14 @@
 
                 @pl.loop(c * span // TILE, (c + 1) * span // TILE, unroll=span // TILE)
                 def _(k):
-                    out_ref[0, at(k), :] = out_ref[0, at(k), :] + wgt[at(k), :] * carry[at(k), :]
+                    stage[0, at(k), :] = stage[0, at(k), :] + wgt[at(k), :] * carry[at(k), :]
 
             @pl.when(t < slices - 1)
             def _():
                 onward[c].start()
 
+            stores[c].start()
+
     fine_step(0, u0, first_halos, lambda: None, between)
     fine_step(1, u1, later_halos, decays, final)
 
@@ -468,6 +476,9 @@
     def _():
         for copy in pieces + onward:
             copy.wait_send()
+
+    for store in stores:
+        store.wait()
 
     for slot in range(2 * FSTEPS):
         everyone(slot, send_s).wait()
@@ -483,14 +494,14 @@
         functools.partial(kernel, slices, n),
         out_shape=jax.ShapeDtypeStruct((1, rows, cols), jnp.float32),
         in_specs=[hbm] * 7,
-        out_specs=pl.BlockSpec(memory_space=pltpu.VMEM),
+        out_specs=hbm,
         scratch_shapes=[
-            grid, grid, pltpu.VMEM((tall, cols), jnp.int32), pltpu.VMEM((2, tall, cols), jnp.float32),
+            pltpu.VMEM((1, rows, cols), jnp.float32), grid, grid, pltpu.VMEM((tall, cols), jnp.int32), pltpu.VMEM((2, tall, cols), jnp.float32),
             *([grid] * 14),
             pltpu.VMEM((rows, cols), jnp.float32),
             pltpu.VMEM((2 * FSTEPS, n, TILE, LANES), jnp.float32),
             *([pltpu.SMEM((REGIONS,), jnp.float32)] * 3),
-            dma((6,)), dma((8,)), dma((8,)), dma((3,)), dma((3,)), dma((CHUNKS,)), dma((CHUNKS,)),
+            dma((6 + CHUNKS,)), dma((8,)), dma((8,)), dma((3,)), dma((3,)), dma((CHUNKS,)), dma((CHUNKS,)),
             dma((2 * FSTEPS,)), dma((2 * FSTEPS,)),
         ],
         compiler_params=pltpu.CompilerParams(

time: 42.4 us -> 41.5 us (0.979)
  Pallas kernels: 40.6 us -> 39.5 us
    pallas_call x1, Pallas kernels: 40.6 us -> 39.5 us  [shards(): pl.pallas_call(functools.partial(kernel, slices, n), out_shape=jax.ShapeD...]
where the time goes in v4:
time: 41.5 us; the launch traced here: 41.2 us
  Pallas kernels  39.5 us (95%)
  local copies, waits for them, and re-layouts  1.67 us (4%)
    pallas_call x1, Pallas kernels, shards(): pl.pallas_call(functools.partial(kernel, slices, n), out_shape=jax.ShapeD...  39.5 us
    unnamed x1, local copies, waits for them, and re-layouts  1.67 us

profile of v4, /device:TPU:0, one launch (start us, length us, event | category | flops | bytes accessed | tf_op | source)
XLA Modules:
  0.0 41.2 jit_solution(13093762661012651804)
XLA Ops:
  0.0 39.5 %shard_map.73 = f32[1,64,1024]{2,1,0:T(8,128)} custom-call(f32[1,64,1024]{2,1,0:T(8,128)} %prev_ref.1, f32[64,1024]{1,0:T(8,128)} %initial_ref.1, f32[2,64,1024]{2,1,0:T(8,128)} %source_ref.1, s32[64,1024]{1,0:T(8,128)} %region_ref.1, f32[4]{0:T(128)} %con_ref.1, f32[4]{0:T(128)} %rel_ref.1, f32[4]{0:T(128)} %sat_ref.1), custom_call_target="tpu_custom_call" | custom-call | tf_op jit(solution)/shard_map/pallas_call | solution.py:493
  39.5 1.7 %copy.9 = f32[1,64,1024]{2,1,0:T(8,128)} copy(f32[1,64,1024]{2,1,0:T(8,128)} %shard_map.73) | data formatting | bytes 524288
